TPU v7x, 32 devices: a whole 2x2x4 slice. The times are simulated.
32 devices in a mesh: depth: 4 (over x, core), row: 4 (over z), col: 2 (over y).
Axes of the slice: x: 2, y: 2, z: 4, core: 2. Of those that a mesh axis runs over, the one named last changes fastest.
Arguments:
- density: float32 [4096, 4096], P('row', ('depth', 'col')), as said below
- pattern: int32 [64, 64], replicated, may hold values from 0 to 1, as said below
- filters: int32 [4, 64, 64], replicated, may hold values from 0 to 1, as said below
Outputs:
- purified: float32 [4096, 4096], P('row', ('depth', 'col'))
Inputs may be any that keep to these rules, and one draw needn't show every extreme that they name: density is symmetric. `pattern`: symmetric 0/1 block table with every diagonal block set. `filters`: each table is a symmetric 0/1 block table with every diagonal block set.
All inputs are finite; a program needn't handle non-finite values.
Results may differ from a plain program's by a relative error of at most 0.007.
Values may be sent and summed in bfloat16 or wider, within the bound.
A program may use at most 64 MiB of HBM per device.

v0:
```python
import jax
import jax.numpy as jnp
from jax import lax
from jax.sharding import PartitionSpec as P

BLK = 64
PURIFY = 2


def spread(value, axis, root):
    mine = lax.axis_index(axis) == root
    return lax.psum(jnp.where(mine, value, jnp.zeros_like(value)), axis)


def on_device(density, pattern, filters):
    rows_wide, seg_width = density.shape
    n_depth = lax.axis_size("depth")
    n_col = lax.axis_size("col")
    layer_index = lax.axis_index("depth")
    row_index = lax.axis_index("row")
    col_index = lax.axis_index("col")
    row_blocks = rows_wide // BLK
    seg_blocks = seg_width // BLK

    def full_mask(keep_table):
        row_strip = lax.dynamic_slice_in_dim(keep_table, row_index * row_blocks, row_blocks, 0)
        groups = row_strip.reshape(row_blocks, n_depth, n_col, seg_blocks)
        picked = lax.dynamic_slice_in_dim(groups, col_index, 1, 2)
        return picked.reshape(row_blocks, n_depth * seg_blocks).astype(jnp.float32)

    def own_mask(keep_table):
        return lax.dynamic_slice_in_dim(
            full_mask(keep_table), layer_index * seg_blocks, seg_blocks, 1
        )

    def apply_mask(values, keep_mask):
        row_count, col_count = keep_mask.shape
        shaped = values.reshape(row_count, BLK, col_count, BLK) * keep_mask[:, None, :, None]
        return shaped.reshape(values.shape)

    def multiply(left_tile, right_side):
        return jnp.dot(
            lax.all_gather(left_tile, "col", axis=1, tiled=True),
            right_side,
            preferred_element_type=jnp.float32,
        )

    def share_layers(partial_sum):
        return lax.psum_scatter(partial_sum, "depth", scatter_dimension=1, tiled=True)

    start_matrix = apply_mask(density, own_mask(pattern))
    current = start_matrix
    for round_index in range(PURIFY):
        operand = current.astype(jnp.bfloat16)
        right_side = spread(
            lax.all_gather(operand, "depth", axis=1, tiled=True), "row", layer_index
        )
        square = apply_mask(
            share_layers(multiply(operand, right_side)), own_mask(filters[2 * round_index])
        )
        cubic = apply_mask(
            share_layers(multiply(square.astype(jnp.bfloat16), right_side)),
            own_mask(filters[2 * round_index + 1]),
        )
        current = 3.0 * square - 2.0 * cubic
    return current


def solution(mesh):
    return jax.shard_map(
        on_device,
        mesh=mesh,
        in_specs=(P("row", ("depth", "col")), P(), P()),
        out_specs=P("row", ("depth", "col")),
        check_vma=False,
    )
```

profile of v0, /device:TPU:0, one launch (start us, length us, event | category | flops | bytes accessed | tf_op | source)
XLA Modules:
  0.0 889.9 jit_solution(13428316623293829066)
XLA Ops:
  6.5 0.8 copy-done
  7.3 0.1 copy.14
  7.4 0.1 copy.5
  7.5 2.3 mul.83
  9.8 3.4 mul.84
  13.2 2.9 multiply_convert_fusion
  16.2 0.7 all-gather.7.cloned.1.call-update
  16.9 36.5 %all-gather.9.cloned.1.call-done = bf16[1024,2048]{1,0:T(8,128)(2,1)} async-done(((bf16[1024,512]{1,0:T(8,128)(2,1)}), bf16[1024,2048]{1,0:T(8,128)(2,1)}) %all-gather.9.cloned.1.call-update) | async-done | bytes 4194320 | tf_op jit(solution)/shard_map/all_gather | solution.py:56
  53.5 4.5 broadcast_select_fusion.1
  58.0 30.2 %all-gather.7.cloned.1.call-done = bf16[1024,1024]{1,0:T(8,128)(2,1)} async-done(((bf16[1024,512]{1,0:T(8,128)(2,1)}), bf16[1024,1024]{1,0:T(8,128)(2,1)}) %all-gather.7.cloned.1.call-update) | async-done | bytes 2097168 | tf_op jit(solution)/shard_map/all_gather | solution.py:43
  88.2 157.4 %all-reduce.3.cloned.1.call-done = bf16[1024,2048]{1,0:T(8,128)(2,1)} async-done(((bf16[1024,2048]{1,0:T(8,128)(2,1)}), bf16[1024,2048]{1,0:T(8,128)(2,1)}) %all-reduce.3.cloned.1.call-update) | async-done | bytes 4194320 | tf_op jit(solution)/shard_map/psum | solution.py:12
  245.5 10.6 %fusion.1 = f32[1024,2048]{1,0:T(8,128)} fusion(bf16[1024,1024]{1,0:T(8,128)(2,1)} %all-gather.7.cloned.1.call-done, bf16[1024,2048]{1,0:T(8,128)(2,1)} %all-reduce.3.cloned.1.call-done), kind=kOutput, calls=%fused_computation.23 | convolution fusion | flops 4294967296 | bytes 14680064 | tf_op jit(solution)/shard_map/dot_general | solution.py:42
  256.2 0.8 copy-done.2
  257.0 0.1 copy.16
  257.1 0.1 copy.7
  257.2 2.3 mul.86
  259.5 3.8 mul.87
  263.3 63.7 %reduce-scatter.5.cloned.1.call-done = f32[1024,512]{1,0:T(8,128)} async-done(((f32[1024,2048]{1,0:T(8,128)}), f32[1024,512]{1,0:T(8,128)}) %reduce-scatter.5.cloned.1.call-update) | async-done | bytes 2097168 | tf_op jit(solution)/shard_map/reduce_scatter | solution.py:49
  327.0 2.9 multiply_convert_fusion.2
  330.0 33.2 %all-gather.11.cloned.1.call-done = bf16[1024,1024]{1,0:T(8,128)(2,1)} async-done(((bf16[1024,512]{1,0:T(8,128)(2,1)}), bf16[1024,1024]{1,0:T(8,128)(2,1)}) %all-gather.11.cloned.1.call-update) | async-done | bytes 2097168 | tf_op jit(solution)/shard_map/all_gather | solution.py:43
  363.2 10.6 %fusion.2 = f32[1024,2048]{1,0:T(8,128)} fusion(bf16[1024,1024]{1,0:T(8,128)(2,1)} %all-gather.11.cloned.1.call-done, bf16[1024,2048]{1,0:T(8,128)(2,1)} %all-reduce.3.cloned.1.call-done), kind=kOutput, calls=%fused_computation.24 | convolution fusion | flops 4294967296 | bytes 14680064 | tf_op jit(solution)/shard_map/dot_general | solution.py:42
  373.8 0.2 all-gather.15.cloned.1.call-start
  374.1 0.1 copy.18
  374.2 0.1 copy.9
  374.2 2.3 mul.90
  376.6 5.0 mul.91
  381.6 64.1 %reduce-scatter.7.cloned.1.call-done = f32[1024,512]{1,0:T(8,128)} async-done(((f32[1024,2048]{1,0:T(8,128)}), f32[1024,512]{1,0:T(8,128)}) %reduce-scatter.7.cloned.1.call-update) | async-done | bytes 2097168 | tf_op jit(solution)/shard_map/reduce_scatter | solution.py:49
  445.7 4.9 subtract_convert_fusion
  450.7 0.7 all-gather.13.cloned.1.call-update
  451.5 33.8 %all-gather.15.cloned.1.call-done = bf16[1024,2048]{1,0:T(8,128)(2,1)} async-done(((bf16[1024,512]{1,0:T(8,128)(2,1)}), bf16[1024,2048]{1,0:T(8,128)(2,1)}) %all-gather.15.cloned.1.call-update) | async-done | bytes 4194320 | tf_op jit(solution)/shard_map/all_gather | solution.py:56
  485.3 4.4 broadcast_select_fusion
  489.8 30.3 %all-gather.13.cloned.1.call-done = bf16[1024,1024]{1,0:T(8,128)(2,1)} async-done(((bf16[1024,512]{1,0:T(8,128)(2,1)}), bf16[1024,1024]{1,0:T(8,128)(2,1)}) %all-gather.13.cloned.1.call-update) | async-done | bytes 2097168 | tf_op jit(solution)/shard_map/all_gather | solution.py:43
  520.1 157.5 %all-reduce.5.cloned.1.call-done = bf16[1024,2048]{1,0:T(8,128)(2,1)} async-done(((bf16[1024,2048]{1,0:T(8,128)(2,1)}), bf16[1024,2048]{1,0:T(8,128)(2,1)}) %all-reduce.5.cloned.1.call-update) | async-done | bytes 4194320 | tf_op jit(solution)/shard_map/psum | solution.py:12
  677.6 10.6 %fusion.3 = f32[1024,2048]{1,0:T(8,128)} fusion(bf16[1024,1024]{1,0:T(8,128)(2,1)} %all-gather.13.cloned.1.call-done, bf16[1024,2048]{1,0:T(8,128)(2,1)} %all-reduce.5.cloned.1.call-done), kind=kOutput, calls=%fused_computation.25 | convolution fusion | flops 4294967296 | bytes 14680064 | tf_op jit(solution)/shard_map/dot_general | solution.py:42
  688.3 0.1 copy.20
  688.4 0.1 copy.11
  688.5 2.3 mul.94
  690.7 3.5 mul.95
  694.3 64.9 %reduce-scatter.9.cloned.1.call-done = f32[1024,512]{1,0:T(8,128)} async-done(((f32[1024,2048]{1,0:T(8,128)}), f32[1024,512]{1,0:T(8,128)}) %reduce-scatter.9.cloned.1.call-update) | async-done | bytes 2097168 | tf_op jit(solution)/shard_map/reduce_scatter | solution.py:49
  759.1 2.9 multiply_convert_fusion.1
  762.1 0.3 reduce-scatter.11.cloned.1.call-start
  762.3 33.0 %all-gather.17.cloned.1.call-done = bf16[1024,1024]{1,0:T(8,128)(2,1)} async-done(((bf16[1024,512]{1,0:T(8,128)(2,1)}), bf16[1024,1024]{1,0:T(8,128)(2,1)}) %all-gather.17.cloned.1.call-update) | async-done | bytes 2097168 | tf_op jit(solution)/shard_map/all_gather | solution.py:43
  795.3 10.6 %fusion.4 = f32[1024,2048]{1,0:T(8,128)} fusion(bf16[1024,1024]{1,0:T(8,128)(2,1)} %all-gather.17.cloned.1.call-done, bf16[1024,2048]{1,0:T(8,128)(2,1)} %all-reduce.5.cloned.1.call-done), kind=kOutput, calls=%fused_computation.26 | convolution fusion | flops 4294967296 | bytes 14680064 | tf_op jit(solution)/shard_map/dot_general | solution.py:42
  805.9 0.1 copy.22
  806.1 2.3 mul.98
  808.4 5.0 mul.99
  813.4 64.4 %reduce-scatter.11.cloned.1.call-done = f32[1024,512]{1,0:T(8,128)} async-done(((f32[1024,2048]{1,0:T(8,128)}), f32[1024,512]{1,0:T(8,128)}) %reduce-scatter.11.cloned.1.call-update) | async-done | bytes 2097168 | tf_op jit(solution)/shard_map/reduce_scatter | solution.py:49
  877.8 5.2 multiply_subtract_fusion
  (39 shorter events, 0.7 us)
Async XLA Ops:
  6.5 0.8 copy-start
  6.5 46.9 %all-gather.9.cloned.1.call-start = ((), (), s32[]{:S(2)}) async-start(), calls=%async_computation.5 | async-start | bytes 5242880 | tf_op jit(solution)/shard_map/all_gather | solution.py:56
  16.1 72.0 %all-gather.7.cloned.1.call-start = ((), (), s32[]{:S(2)}) async-start(), calls=%async_computation.4 | async-start | bytes 3145728 | tf_op jit(solution)/shard_map/all_gather | solution.py:43
  16.9 228.7 %all-reduce.3.cloned.1.call-start = ((), (), s32[]{:S(2)}) async-start(), calls=%async_computation.6 | async-start | bytes 8388608 | tf_op jit(solution)/shard_map/psum | solution.py:12
  57.9 269.1 %reduce-scatter.5.cloned.1.call-start = ((), (), s32[]{:S(2)}) async-start(), calls=%async_computation.7 | async-start | bytes 10485760 | tf_op jit(solution)/shard_map/reduce_scatter | solution.py:49
  256.1 0.9 copy-start.2
  256.1 107.1 %all-gather.11.cloned.1.call-start = ((), (), s32[]{:S(2)}) async-start(), calls=%async_computation.8 | async-start | bytes 3145728 | tf_op jit(solution)/shard_map/all_gather | solution.py:43
  329.9 115.8 %reduce-scatter.7.cloned.1.call-start = ((), (), s32[]{:S(2)}) async-start(), calls=%async_computation.9 | async-start | bytes 10485760 | tf_op jit(solution)/shard_map/reduce_scatter | solution.py:49
  373.8 111.5 %all-gather.15.cloned.1.call-start = ((), (), s32[]{:S(2)}) async-start(), calls=%async_computation.11 | async-start | bytes 5242880 | tf_op jit(solution)/shard_map/all_gather | solution.py:56
  450.7 69.4 %all-gather.13.cloned.1.call-start = ((), (), s32[]{:S(2)}) async-start(), calls=%async_computation.10 | async-start | bytes 3145728 | tf_op jit(solution)/shard_map/all_gather | solution.py:43
  451.4 226.2 %all-reduce.5.cloned.1.call-start = ((), (), s32[]{:S(2)}) async-start(), calls=%async_computation.12 | async-start | bytes 8388608 | tf_op jit(solution)/shard_map/psum | solution.py:12
  489.8 269.4 %reduce-scatter.9.cloned.1.call-start = ((), (), s32[]{:S(2)}) async-start(), calls=%async_computation.13 | async-start | bytes 10485760 | tf_op jit(solution)/shard_map/reduce_scatter | solution.py:49
  688.2 107.1 %all-gather.17.cloned.1.call-start = ((), (), s32[]{:S(2)}) async-start(), calls=%async_computation.14 | async-start | bytes 3145728 | tf_op jit(solution)/shard_map/all_gather | solution.py:43
  762.1 115.8 %reduce-scatter.11.cloned.1.call-start = ((), (), s32[]{:S(2)}) async-start(), calls=%async_computation.15 | async-start | bytes 10485760 | tf_op jit(solution)/shard_map/reduce_scatter | solution.py:49
  877.8 5.2 copy-start.1
Sparse Core Ops, SparseCore 0:
  16.2 37.1 all-gather.8
  55.0 33.1 all-gather.6
  90.5 154.9 all-reduce.2
  256.3 70.7 reduce-scatter.4
  330.1 33.1 all-gather.10
  373.9 71.7 reduce-scatter.6
  450.8 34.4 all-gather.14
  486.9 33.1 all-gather.12
  522.6 154.9 all-reduce.4
  688.3 70.7 reduce-scatter.8
  762.2 33.1 all-gather.16
  806.1 71.7 reduce-scatter.10
where the time goes:
time: 891 us; the launch traced here: 890 us
  waiting for transfers between devices  771 us (87%)
  matrix products  42.3 us (5%)
  local copies, waits for them, and re-layouts  34.7 us (4%)
  other arithmetic  27.8 us (3%)
  between operations  13.7 us (2%)
    psum x2, waiting for transfers between devices, spread(): return lax.psum(jnp.where(mine, value, jnp.zeros_like(value)), axis)  315 us
    reduce_scatter x4, waiting for transfers between devices, share_layers(): lax.psum_scatter(partial_sum, 'depth', scatter_dimension=1, tiled=True)  257 us
    all_gather x4, waiting for transfers between devices, multiply(): lax.all_gather(left_tile, 'col', axis=1, tiled=True)  127 us
    all_gather x2, waiting for transfers between devices, on_device(): lax.all_gather(operand, 'depth', axis=1, tiled=True)  70.4 us
    dot_general x4, matrix products, multiply(): jnp.dot(lax.all_gather(left_tile, 'col', axis=1, tiled=True), right_side,...  42.3 us
    mul x10, local copies, waits for them, and re-layouts, apply_mask(): values.reshape(row_count, BLK, col_count, BLK) * keep_mask[:, None, :, None]  32.3 us
  transfers between devices with their start and end apart: 12, of which 12 were waited for; matrix products, arithmetic and copies ran while one was open for 4% of the time, Pallas kernels for 0%

commit v1 on v0

--- a/solution.py
+++ b/solution.py
@@ -9,7 +9,7 @@
 
 def spread(value, axis, root):
     mine = lax.axis_index(axis) == root
-    return lax.psum(jnp.where(mine, value, jnp.zeros_like(value)), axis)
+    return jnp.sum(lax.all_gather(jnp.where(mine, value, jnp.zeros_like(value)), axis), axis=0)
 
 
 def on_device(density, pattern, filters):

time: 891 us -> 1160 us (1.30)
  waiting for transfers between devices: 771 us -> 1010 us
  other arithmetic: 27.8 us -> 52.6 us
    all_gather x0 -> x2, waiting for transfers between devices: none -> 572 us  [spread(): lax.all_gather(jnp.where(mine, value, jnp.zeros_like(value)), axis)]
    psum x2 -> x0, waiting for transfers between devices: 315 us -> none  [spread(): return lax.psum(jnp.where(mine, value, jnp.zeros_like(value)), axis)]
    reduce_sum x0 -> x2, other arithmetic: none -> 24.9 us  [spread(): jnp.sum(lax.all_gather(jnp.where(mine, value, jnp.zeros_like(value)), axi...]
    all_gather x4, waiting for transfers between devices: 127 us -> 107 us  [multiply(): lax.all_gather(left_tile, 'col', axis=1, tiled=True)]
  transfers between devices with their start and end apart: 12 -> 12, of which waited for: 12 -> 12; matrix products, arithmetic and copies ran while one was open for 4% -> 5% of each run, Pallas kernels for 0% -> 0%
where the time goes in v1:
time: 1160 us
  waiting for transfers between devices  1010 us (87%)
  other arithmetic  52.6 us (5%)
  matrix products  42.3 us (4%)
  local copies, waits for them, and re-layouts  34.6 us (3%)
  between operations  13.7 us (1%)
    all_gather x2, waiting for transfers between devices, spread(): lax.all_gather(jnp.where(mine, value, jnp.zeros_like(value)), axis)  572 us
    reduce_scatter x4, waiting for transfers between devices, share_layers(): lax.psum_scatter(partial_sum, 'depth', scatter_dimension=1, tiled=True)  259 us
    all_gather x4, waiting for transfers between devices, multiply(): lax.all_gather(left_tile, 'col', axis=1, tiled=True)  107 us
    all_gather x2, waiting for transfers between devices, on_device(): lax.all_gather(operand, 'depth', axis=1, tiled=True)  71.9 us
    dot_general x4, matrix products, multiply(): jnp.dot(lax.all_gather(left_tile, 'col', axis=1, tiled=True), right_side,...  42.3 us
    mul x10, local copies, waits for them, and re-layouts, apply_mask(): values.reshape(row_count, BLK, col_count, BLK) * keep_mask[:, None, :, None]  32.2 us
    reduce_sum x2, other arithmetic, spread(): jnp.sum(lax.all_gather(jnp.where(mine, value, jnp.zeros_like(value)), axi...  24.9 us
  transfers between devices with their start and end apart: 12, of which 12 were waited for; matrix products, arithmetic and copies ran while one was open for 5% of the time, Pallas kernels for 0%

profile of v1, /device:TPU:0, one launch (start us, length us, event | category | flops | bytes accessed | tf_op | source)
XLA Modules:
  0.0 1155.8 jit_solution(8255825628038279232)
XLA Ops:
  6.5 0.8 copy-done
  7.3 0.1 copy.14
  7.4 0.1 copy.5
  7.5 2.3 mul.83
  9.8 3.4 mul.84
  13.2 2.9 multiply_convert_fusion
  16.2 37.3 %all-gather.13.cloned.1.call-done = bf16[1024,2048]{1,0:T(8,128)(2,1)} async-done(((bf16[1024,512]{1,0:T(8,128)(2,1)}), bf16[1024,2048]{1,0:T(8,128)(2,1)}) %all-gather.13.cloned.1.call-update) | async-done | bytes 4194320 | tf_op jit(solution)/shard_map/all_gather | solution.py:56
  53.5 4.4 broadcast_select_fusion.1
  57.9 0.7 all-gather.11.cloned.1.call-update
  58.7 286.0 %all-gather.23.cloned.1.call-done = bf16[4096,2048]{1,0:T(8,128)(2,1)} async-done(((bf16[1024,2048]{1,0:T(8,128)(2,1)}), bf16[4096,2048]{1,0:T(8,128)(2,1)}) %all-gather.23.cloned.1.call-update) | async-done | bytes 16777232 | tf_op jit(solution)/shard_map/all_gather | solution.py:12
  344.7 12.4 %reduce_sum.24 = bf16[1024,2048]{1,0:T(8,128)(2,1)} reduce(bf16[4,1024,2048]{2,1,0:T(8,128)(2,1)} %bitcast.36, bf16[]{:T(256)} %constant.33.clone.1), dimensions={0}, to_apply=%region_0.1 | reduce | flops 6291456 | bytes 20971522 | tf_op jit(solution)/shard_map/reduce_sum | solution.py:12
  357.2 20.4 %all-gather.11.cloned.1.call-done = bf16[1024,1024]{1,0:T(8,128)(2,1)} async-done(((bf16[1024,512]{1,0:T(8,128)(2,1)}), bf16[1024,1024]{1,0:T(8,128)(2,1)}) %all-gather.11.cloned.1.call-update) | async-done | bytes 2097168 | tf_op jit(solution)/shard_map/all_gather | solution.py:43
  377.6 10.6 fusion.1
  388.3 0.8 copy-done.2
  389.1 0.1 copy.16
  389.2 0.1 copy.7
  389.3 2.3 mul.86
  391.6 3.6 mul.87
  395.2 64.9 %reduce-scatter.5.cloned.1.call-done = f32[1024,512]{1,0:T(8,128)} async-done(((f32[1024,2048]{1,0:T(8,128)}), f32[1024,512]{1,0:T(8,128)}) %reduce-scatter.5.cloned.1.call-update) | async-done | bytes 2097168 | tf_op jit(solution)/shard_map/reduce_scatter | solution.py:49
  460.1 2.9 multiply_convert_fusion.2
  463.1 33.2 %all-gather.15.cloned.1.call-done = bf16[1024,1024]{1,0:T(8,128)(2,1)} async-done(((bf16[1024,512]{1,0:T(8,128)(2,1)}), bf16[1024,1024]{1,0:T(8,128)(2,1)}) %all-gather.15.cloned.1.call-update) | async-done | bytes 2097168 | tf_op jit(solution)/shard_map/all_gather | solution.py:43
  496.3 10.6 fusion.2
  506.9 0.2 all-gather.19.cloned.1.call-start
  507.1 0.1 copy.18
  507.3 2.3 mul.90
  509.6 5.0 mul.91
  514.7 64.2 %reduce-scatter.7.cloned.1.call-done = f32[1024,512]{1,0:T(8,128)} async-done(((f32[1024,2048]{1,0:T(8,128)}), f32[1024,512]{1,0:T(8,128)}) %reduce-scatter.7.cloned.1.call-update) | async-done | bytes 2097168 | tf_op jit(solution)/shard_map/reduce_scatter | solution.py:49
  578.8 4.9 subtract_convert_fusion
  583.8 34.6 %all-gather.19.cloned.1.call-done = bf16[1024,2048]{1,0:T(8,128)(2,1)} async-done(((bf16[1024,512]{1,0:T(8,128)(2,1)}), bf16[1024,2048]{1,0:T(8,128)(2,1)}) %all-gather.19.cloned.1.call-update) | async-done | bytes 4194320 | tf_op jit(solution)/shard_map/all_gather | solution.py:56
  618.4 4.4 broadcast_select_fusion
  622.9 0.7 all-gather.17.cloned.1.call-update
  623.6 286.0 %all-gather.25.cloned.1.call-done = bf16[4096,2048]{1,0:T(8,128)(2,1)} async-done(((bf16[1024,2048]{1,0:T(8,128)(2,1)}), bf16[4096,2048]{1,0:T(8,128)(2,1)}) %all-gather.25.cloned.1.call-update) | async-done | bytes 16777232 | tf_op jit(solution)/shard_map/all_gather | solution.py:12
  909.6 12.4 %reduce_sum.25 = bf16[1024,2048]{1,0:T(8,128)(2,1)} reduce(bf16[4,1024,2048]{2,1,0:T(8,128)(2,1)} %bitcast.35, bf16[]{:T(256)} %constant.33.clone.1), dimensions={0}, to_apply=%region_3.4 | reduce | flops 6291456 | bytes 20971522 | tf_op jit(solution)/shard_map/reduce_sum | solution.py:12
  922.1 20.4 %all-gather.17.cloned.1.call-done = bf16[1024,1024]{1,0:T(8,128)(2,1)} async-done(((bf16[1024,512]{1,0:T(8,128)(2,1)}), bf16[1024,1024]{1,0:T(8,128)(2,1)}) %all-gather.17.cloned.1.call-update) | async-done | bytes 2097168 | tf_op jit(solution)/shard_map/all_gather | solution.py:43
  942.5 10.6 fusion.3
  953.2 0.1 copy.20
  953.4 2.3 mul.94
  955.7 3.6 mul.95
  959.3 65.8 %reduce-scatter.9.cloned.1.call-done = f32[1024,512]{1,0:T(8,128)} async-done(((f32[1024,2048]{1,0:T(8,128)}), f32[1024,512]{1,0:T(8,128)}) %reduce-scatter.9.cloned.1.call-update) | async-done | bytes 2097168 | tf_op jit(solution)/shard_map/reduce_scatter | solution.py:49
  1025.1 2.9 multiply_convert_fusion.1
  1028.0 0.3 reduce-scatter.11.cloned.1.call-start
  1028.3 33.0 %all-gather.21.cloned.1.call-done = bf16[1024,1024]{1,0:T(8,128)(2,1)} async-done(((bf16[1024,512]{1,0:T(8,128)(2,1)}), bf16[1024,1024]{1,0:T(8,128)(2,1)}) %all-gather.21.cloned.1.call-update) | async-done | bytes 2097168 | tf_op jit(solution)/shard_map/all_gather | solution.py:43
  1061.3 10.6 fusion.4
  1071.9 0.1 copy.22
  1072.0 2.3 mul.98
  1074.4 5.0 mul.99
  1079.4 64.4 %reduce-scatter.11.cloned.1.call-done = f32[1024,512]{1,0:T(8,128)} async-done(((f32[1024,2048]{1,0:T(8,128)}), f32[1024,512]{1,0:T(8,128)}) %reduce-scatter.11.cloned.1.call-update) | async-done | bytes 2097168 | tf_op jit(solution)/shard_map/reduce_scatter | solution.py:49
  1143.8 5.2 multiply_subtract_fusion
  (41 shorter events, 0.9 us)
Async XLA Ops:
  6.5 0.8 copy-start
  6.5 46.9 %all-gather.13.cloned.1.call-start = ((), (), s32[]{:S(2)}) async-start(), calls=%async_computation.5 | async-start | bytes 5242880 | tf_op jit(solution)/shard_map/all_gather | solution.py:56
  16.1 328.6 %all-gather.23.cloned.1.call-start = ((), (), s32[]{:S(2)}) async-start(), calls=%async_computation.14 | async-start | bytes 20971520 | tf_op jit(solution)/shard_map/all_gather | solution.py:12
  57.9 319.7 %all-gather.11.cloned.1.call-start = ((), (), s32[]{:S(2)}) async-start(), calls=%async_computation.4 | async-start | bytes 3145728 | tf_op jit(solution)/shard_map/all_gather | solution.py:43
  58.6 401.5 %reduce-scatter.5.cloned.1.call-start = ((), (), s32[]{:S(2)}) async-start(), calls=%async_computation.6 | async-start | bytes 10485760 | tf_op jit(solution)/shard_map/reduce_scatter | solution.py:49
  388.2 0.9 copy-start.2
  388.2 108.1 %all-gather.15.cloned.1.call-start = ((), (), s32[]{:S(2)}) async-start(), calls=%async_computation.7 | async-start | bytes 3145728 | tf_op jit(solution)/shard_map/all_gather | solution.py:43
  463.0 115.8 %reduce-scatter.7.cloned.1.call-start = ((), (), s32[]{:S(2)}) async-start(), calls=%async_computation.8 | async-start | bytes 10485760 | tf_op jit(solution)/shard_map/reduce_scatter | solution.py:49
  506.9 111.5 %all-gather.19.cloned.1.call-start = ((), (), s32[]{:S(2)}) async-start(), calls=%async_computation.10 | async-start | bytes 5242880 | tf_op jit(solution)/shard_map/all_gather | solution.py:56
  583.7 325.9 %all-gather.25.cloned.1.call-start = ((), (), s32[]{:S(2)}) async-start(), calls=%async_computation.15 | async-start | bytes 20971520 | tf_op jit(solution)/shard_map/all_gather | solution.py:12
  622.8 319.7 %all-gather.17.cloned.1.call-start = ((), (), s32[]{:S(2)}) async-start(), calls=%async_computation.9 | async-start | bytes 3145728 | tf_op jit(solution)/shard_map/all_gather | solution.py:43
  623.6 401.5 %reduce-scatter.9.cloned.1.call-start = ((), (), s32[]{:S(2)}) async-start(), calls=%async_computation.11 | async-start | bytes 10485760 | tf_op jit(solution)/shard_map/reduce_scatter | solution.py:49
  953.1 108.1 %all-gather.21.cloned.1.call-start = ((), (), s32[]{:S(2)}) async-start(), calls=%async_computation.12 | async-start | bytes 3145728 | tf_op jit(solution)/shard_map/all_gather | solution.py:43
  1028.0 115.8 %reduce-scatter.11.cloned.1.call-start = ((), (), s32[]{:S(2)}) async-start(), calls=%async_computation.13 | async-start | bytes 10485760 | tf_op jit(solution)/shard_map/reduce_scatter | solution.py:49
  1143.8 5.2 copy-start.1
Sparse Core Ops, SparseCore 0:
  16.2 37.1 all-gather.12
  58.0 286.6 all-gather.22
  346.3 31.2 all-gather.10
  388.3 71.7 reduce-scatter.4
  463.1 33.1 all-gather.14
  507.0 71.7 reduce-scatter.6
  583.9 34.4 all-gather.18
  622.9 286.6 all-gather.24
  911.2 31.2 all-gather.16
  953.3 71.7 reduce-scatter.8
  1028.1 33.1 all-gather.20
  1072.0 71.7 reduce-scatter.10
